TPU v7x, 128 devices: a whole 4x4x4 slice. The times are simulated.
128 devices in a mesh: seq: 8 (over y, core), pool: 16 (over x, z).
Axes of the slice: x: 4, y: 4, z: 4, core: 2. Of those that a mesh axis runs over, the one named last changes fastest.
Arguments:
- queries: bfloat16 [16, 4096, 4096], P('pool', 'seq'), may hold values from -6.5 to 6.5
- text_kv: bfloat16 [16, 4096, 1024], P('pool', 'seq'), may hold values from -6 to 6
- tile_embeds: bfloat16 [8, 2048, 8192], P('seq', 'pool'), may hold values from -400 to 400
- stored_kv: bfloat16 [8, 4096, 1024], P('seq', 'pool'), may hold values from -6 to 6
- w_kv: bfloat16 [8192, 1024], P('pool'), may hold values from -0.0625 to 0.0625
- block_source: int32 [16, 128], P(None, 'seq'), may hold values from 0 to 192, as said below
- block_mask: int32 [16, 128, 128], P('pool'), may hold values 0 or 1
Outputs:
- attended: bfloat16 [16, 4096, 4096], P('pool', 'seq')
Inputs may be any that keep to these rules, and one draw needn't show every extreme that they name: `block_source`: At most 2 blocks of one sequence shard of one request come from one device, and some shard reaches that in every draw. Each miss tile is named at most once; a cached block may be named by several requests.
All inputs are finite; a program needn't handle non-finite values. No bound on the sum of `block_mask` on one device may be relied on, other than what follows from the above.
Results may differ from a plain program's by a relative error of at most 0.013.
Values may be sent and summed in bfloat16 or wider, within the bound.
No kernel may reach another device: no remote copies, remote signals or barrier semaphores. Data moves between devices by JAX's collectives and lax.ppermute only.
A program may use at most 192 MiB of HBM per device.

v0:
```python
import jax
import jax.numpy as jnp
from jax import lax
from jax.sharding import PartitionSpec as P

HEAD_SIZE = 128
BLOCK_ROWS = 32
SOURCE_CAP = 2


big_negative = -1e30
eps_norm = 1e-06


def head_update(
    carried, query_rows, positions, mask_rows, key_rows, value_rows, key_start, block_rows
):
    row_max, denominator, summed = carried
    key_count = key_rows.shape[0]
    key_pos = key_start + lax.iota(jnp.int32, key_count)
    scores = jnp.einsum(
        "qhgd,khd->hgqk", query_rows, key_rows, preferred_element_type=jnp.float32
    ) * key_rows.shape[-1] ** (-0.5)
    mask_cols = lax.dynamic_slice_in_dim(
        mask_rows, key_start // block_rows, key_count // block_rows, 1
    )
    mask_cols = jnp.repeat(mask_cols, block_rows, axis=1)
    query_block = positions // block_rows
    key_block = key_pos // block_rows
    allowed = (key_pos[None, :] <= positions[:, None]) & (
        (key_block[None, :] == query_block[:, None]) | (mask_cols == 1)
    )
    scores = jnp.where(allowed, scores, big_negative)
    new_max = jnp.maximum(row_max, jnp.max(scores, axis=-1))
    factor = jnp.exp(row_max - new_max)
    weights = jnp.where(allowed, jnp.exp(scores - new_max[..., None]), 0.0)
    denominator = denominator * factor + jnp.sum(weights, axis=-1)
    summed = summed * factor[..., None] + jnp.einsum(
        "hgqk,khd->hgqd",
        weights.astype(jnp.bfloat16),
        value_rows,
        preferred_element_type=jnp.float32,
    )
    return (new_max, denominator, summed)


def visit_groups(carried, key_part, key_start, groups, block_rows, kv_width):
    key_count = key_part.shape[0]
    head_size = groups[0][0].shape[-1]
    key_rows = key_part[:, :kv_width].reshape(key_count, -1, head_size)
    value_rows = key_part[:, kv_width:].reshape(key_count, -1, head_size)
    query_rows, positions, mask_rows = groups[0]

    def compute(old_state, query_rows=query_rows, positions=positions, mask_rows=mask_rows):
        return head_update(
            old_state, query_rows, positions, mask_rows, key_rows, value_rows, key_start, block_rows
        )

    def keep_state(old_state):
        return old_state

    updated = [lax.cond(key_start <= jnp.max(positions), compute, keep_state, carried[0])]
    return tuple(updated)


def body(queries, text_kv, tile_embeds, stored_kv, w_kv, block_source, block_mask):
    pool_count = lax.axis_size("pool")
    my_pool = lax.axis_index("pool")
    my_seq = lax.axis_index("seq")
    shard_tokens = queries.shape[1]
    kv_width = text_kv.shape[2] // 2
    block_rows = BLOCK_ROWS
    source_cap = SOURCE_CAP
    shard_blocks = shard_tokens // block_rows
    store_slots = stored_kv.shape[1] // block_rows
    tile_slots = tile_embeds.shape[1] // block_rows
    entries = store_slots + tile_slots
    tiles_f32 = tile_embeds[0].astype(jnp.float32)
    mean_square = jnp.mean(tiles_f32 * tiles_f32, axis=-1, keepdims=True)
    normed = (tiles_f32 * lax.rsqrt(mean_square + eps_norm)).astype(jnp.bfloat16)
    encoded = jnp.dot(
        normed, lax.all_gather(w_kv, "pool", axis=0, tiled=True), preferred_element_type=jnp.float32
    )
    encoded = encoded.astype(jnp.bfloat16).reshape(tile_slots, block_rows, 2 * kv_width)
    block_table = jnp.concatenate(
        [stored_kv[0].reshape(store_slots, block_rows, 2 * kv_width), encoded], axis=0
    )
    is_image = block_source > 0
    source_index = jnp.maximum(block_source - 1, 0)
    source_pool = source_index // entries
    entry_index = source_index % entries
    outgoing = is_image & (source_pool == my_pool)
    order_rank = jnp.cumsum(outgoing.astype(jnp.int32), axis=1) - 1
    slot_ids = lax.iota(jnp.int32, source_cap)
    selected = outgoing[:, None, :] & (order_rank[:, None, :] == slot_ids[None, :, None])
    picked_entry = jnp.sum(jnp.where(selected, entry_index[:, None, :], 0), axis=2)
    slot_used = jnp.any(selected, axis=2)
    sending = jnp.take(block_table, picked_entry.reshape(-1), axis=0, mode="clip")
    sending = jnp.where(slot_used.reshape(-1)[:, None, None], sending, jnp.zeros_like(sending))
    sending = sending.reshape(-1, 2 * kv_width)
    arrived = lax.all_to_all(sending, "pool", split_axis=0, concat_axis=0, tiled=True)
    arrived = arrived.reshape(pool_count * source_cap, block_rows, 2 * kv_width)
    my_codes = lax.dynamic_index_in_dim(block_source, my_pool, 0, keepdims=False)
    my_image = my_codes > 0
    my_source = jnp.maximum(my_codes - 1, 0) // entries
    block_order = lax.iota(jnp.int32, shard_blocks)
    same_source = (
        my_image[None, :]
        & (my_source[None, :] == my_source[:, None])
        & (block_order[None, :] < block_order[:, None])
    )
    my_rank = jnp.sum(same_source.astype(jnp.int32), axis=1)
    fetched = jnp.take(arrived, my_source * source_cap + my_rank, axis=0, mode="clip")
    local_blocks = text_kv[0].reshape(shard_blocks, block_rows, 2 * kv_width)
    assembled = jnp.where(my_image[:, None, None], fetched, local_blocks).reshape(
        shard_tokens, 2 * kv_width
    )
    head_size = HEAD_SIZE
    key_heads = kv_width // head_size
    query_heads = queries.shape[2] // head_size
    group_size = query_heads // key_heads
    mask_table = block_mask[0]
    own_queries = queries[0]
    base_position = my_seq * shard_tokens

    def empty_state(row_count):
        return (
            jnp.full((key_heads, group_size, row_count), big_negative, jnp.float32),
            jnp.zeros((key_heads, group_size, row_count), jnp.float32),
            jnp.zeros((key_heads, group_size, row_count, head_size), jnp.float32),
        )

    positions = base_position + lax.iota(jnp.int32, shard_tokens)
    shaped = own_queries.reshape(own_queries.shape[0], key_heads, group_size, head_size)
    mask_rows = jnp.take(mask_table, positions // block_rows, axis=0)
    groups = ((shaped, positions, mask_rows),)
    starting = tuple((empty_state(one_group[0].shape[0]) for one_group in groups))
    key_piece = lax.all_gather(assembled, "seq", axis=0, tiled=True)
    piece_blocks = key_piece.shape[0] // shard_tokens

    def one_block(block_index, inner_state):
        key_part = lax.dynamic_slice_in_dim(key_piece, block_index * shard_tokens, shard_tokens, 0)
        return visit_groups(
            inner_state, key_part, block_index * shard_tokens, groups, block_rows, kv_width
        )

    finished = lax.fori_loop(0, piece_blocks, one_block, starting)
    row_max, denominator, summed = finished[0]
    result = summed / denominator[..., None]
    attended = jnp.transpose(result, (2, 0, 1, 3)).reshape(result.shape[2], -1).astype(jnp.bfloat16)
    return attended[None]


def solution(mesh):
    return jax.shard_map(
        body,
        mesh=mesh,
        in_specs=(
            P("pool", "seq", None),
            P("pool", "seq", None),
            P("seq", "pool", None),
            P("seq", "pool", None),
            P("pool", None),
            P(None, "seq"),
            P("pool", None, None),
        ),
        out_specs=P("pool", "seq", None),
        check_vma=False,
    )
```

profile of v0, /device:TPU:27, one launch (start us, length us, event | category | flops | bytes accessed | tf_op | source)
XLA Modules:
  0.0 690.0 jit_solution(16267075402365032062)
XLA Ops:
  11.7 111.4 %all-gather.3.cloned.1.call-done = bf16[8192,1024]{1,0:T(8,128)(2,1)} async-done(((bf16[512,1024]{1,0:T(8,128)(2,1)}), bf16[8192,1024]{1,0:T(8,128)(2,1)}) %all-gather.3.cloned.1.call-update) | async-done | bytes 16777232 | tf_op jit(solution)/shard_map/all_gather | solution.py:82
  141.2 23.1 %all-to-all-done = bf16[16,64,1024]{2,1,0:T(8,128)(2,1)S(1)} async-done(((bf16[16,64,1024]{2,1,0:T(8,128)(2,1)}), bf16[16,64,1024]{2,1,0:T(8,128)(2,1)S(1)}, u32[]{:S(2)}, u32[]{:S(2)}) %all-to-all-start) | async-done | bytes 2097184 | tf_op jit(solution)/shard_map/all_to_all | solution.py:101
  182.3 37.0 %all-gather.5.cloned.1.call-done = bf16[4096,1024]{1,0:T(8,128)(2,1)} async-done(((bf16[512,1024]{1,0:T(8,128)(2,1)}), bf16[4096,1024]{1,0:T(8,128)(2,1)}) %all-gather.5.cloned.1.call-update) | async-done | bytes 8388624 | tf_op jit(solution)/shard_map/all_gather | solution.py:138
  235.0 431.0 %while.19 = (s32[]{:T(128)}, f32[4,8,512]{2,1,0:T(8,128)S(1)}, f32[4,8,512]{2,1,0:T(8,128)S(1)}, f32[4,8,512,128]{3,2,1,0:T(8,128)}, s32[]{:T(128)}, /*index=5*/...) while((s32[]{:T(128)}, f32[4,8,512]{2,1,0:T(8,128)S(1)}, ...), condition=%wide.region_11.12_spmd.clone, body=%wide.region_6.11_spmd.clone.sunk | while | flops 4409319936 | bytes 185668176 | solution.py:147
  235.6 53.3 %conditional.3 = ((f32[4,8,512]{2,1,0:T(8,128)S(1)}, f32[4,8,512]{2,1,0:T(8,128)S(1)}, f32[4,8,512,128]{3,2,1,0:T(8,128)})) conditional(s32[]{:T(128)} %convert_element_type.73, (f32[4,8,512]{2,1,0:T(8,128)S(1)}, f32[4,8,512]{2,1,0:T(8,128)S(1)}, f32[4,8,512,128]{3,2,1,0:T(8,128)}) %tuple.65, (s32[]{:T(128)}, s32[]{:T(128)}, ...), branch_computations={%region_7.7_spmd, %region_8.10_spmd} | conditional | flops 4409319936 | bytes 185665888 | solution.py:62
  237.5 16.1 %fusion.2 = (f32[4,8,512]{2,1,0:T(8,128)S(1)}, f32[4,512,512,8]{2,1,3,0:T(8,128)}) fusion(pred[512,512]{0,1:T(8,128)(4,1)S(1)} %fusion.10, bf16[512,4,128,1]{0,2,3,1:T(8,128)(2,1)S(1)} %bitcast.84, bf16[512,4,8,128]{3,0,2,1:T(8,128)(2,1)} %get-tuple-element.265), kind=kOutput, calls=%fused_computation.6 | convolution fusion | flops 2172633088 | bytes 38600704 | tf_op jit(solution)/shard_map/while/body/eval_jaxpr/cond/branch_1_fun/qhgd,khd->hgqk/dot_general | solution.py:21
  268.7 16.9 %multiply_add_fusion = f32[4,8,512,128]{3,2,1,0:T(8,128)S(1)} fusion(f32[4,8,512,128]{3,2,1,0:T(8,128)S(1)} %bitcast.86, f32[4,8,512]{2,1,0:T(8,128)S(1)} %get-tuple-element.367, bf16[512,4,128,1]{0,2,3,1:T(8,128)(2,1)S(1)} %bitcast.88, f32[4,512,512,8]{2,1,3,0:T(8,128)} %get-tuple-element.378, f32[4,8,512]{2,1,0:T(8,128)S(1)} %max.21, ...), kind=kOutput, calls=%fused_computation.11 | convolution fusion | flops 2193620992 | bytes 51249152 | tf_op jit(solution)/shard_map/while/body/eval_jaxpr/cond/branch_1_fun/hgqk,khd->hgqd/dot_general | solution.py:38
  289.5 53.3 %conditional.3 = ((f32[4,8,512]{2,1,0:T(8,128)S(1)}, f32[4,8,512]{2,1,0:T(8,128)S(1)}, f32[4,8,512,128]{3,2,1,0:T(8,128)})) conditional(s32[]{:T(128)} %convert_element_type.73, (f32[4,8,512]{2,1,0:T(8,128)S(1)}, f32[4,8,512]{2,1,0:T(8,128)S(1)}, f32[4,8,512,128]{3,2,1,0:T(8,128)}) %tuple.65, (s32[]{:T(128)}, s32[]{:T(128)}, ...), branch_computations={%region_7.7_spmd, %region_8.10_spmd} | conditional | flops 4409319936 | bytes 185665888 | solution.py:62
  291.4 16.1 %fusion.2 = (f32[4,8,512]{2,1,0:T(8,128)S(1)}, f32[4,512,512,8]{2,1,3,0:T(8,128)}) fusion(pred[512,512]{0,1:T(8,128)(4,1)S(1)} %fusion.10, bf16[512,4,128,1]{0,2,3,1:T(8,128)(2,1)S(1)} %bitcast.84, bf16[512,4,8,128]{3,0,2,1:T(8,128)(2,1)} %get-tuple-element.265), kind=kOutput, calls=%fused_computation.6 | convolution fusion | flops 2172633088 | bytes 38600704 | tf_op jit(solution)/shard_map/while/body/eval_jaxpr/cond/branch_1_fun/qhgd,khd->hgqk/dot_general | solution.py:21
  322.6 16.9 %multiply_add_fusion = f32[4,8,512,128]{3,2,1,0:T(8,128)S(1)} fusion(f32[4,8,512,128]{3,2,1,0:T(8,128)S(1)} %bitcast.86, f32[4,8,512]{2,1,0:T(8,128)S(1)} %get-tuple-element.367, bf16[512,4,128,1]{0,2,3,1:T(8,128)(2,1)S(1)} %bitcast.88, f32[4,512,512,8]{2,1,3,0:T(8,128)} %get-tuple-element.378, f32[4,8,512]{2,1,0:T(8,128)S(1)} %max.21, ...), kind=kOutput, calls=%fused_computation.11 | convolution fusion | flops 2193620992 | bytes 51249152 | tf_op jit(solution)/shard_map/while/body/eval_jaxpr/cond/branch_1_fun/hgqk,khd->hgqd/dot_general | solution.py:38
  343.4 53.2 %conditional.3 = ((f32[4,8,512]{2,1,0:T(8,128)S(1)}, f32[4,8,512]{2,1,0:T(8,128)S(1)}, f32[4,8,512,128]{3,2,1,0:T(8,128)})) conditional(s32[]{:T(128)} %convert_element_type.73, (f32[4,8,512]{2,1,0:T(8,128)S(1)}, f32[4,8,512]{2,1,0:T(8,128)S(1)}, f32[4,8,512,128]{3,2,1,0:T(8,128)}) %tuple.65, (s32[]{:T(128)}, s32[]{:T(128)}, ...), branch_computations={%region_7.7_spmd, %region_8.10_spmd} | conditional | flops 4409319936 | bytes 185665888 | solution.py:62
  376.5 16.9 %multiply_add_fusion = f32[4,8,512,128]{3,2,1,0:T(8,128)S(1)} fusion(f32[4,8,512,128]{3,2,1,0:T(8,128)S(1)} %bitcast.86, f32[4,8,512]{2,1,0:T(8,128)S(1)} %get-tuple-element.367, bf16[512,4,128,1]{0,2,3,1:T(8,128)(2,1)S(1)} %bitcast.88, f32[4,512,512,8]{2,1,3,0:T(8,128)} %get-tuple-element.378, f32[4,8,512]{2,1,0:T(8,128)S(1)} %max.21, ...), kind=kOutput, calls=%fused_computation.11 | convolution fusion | flops 2193620992 | bytes 51249152 | tf_op jit(solution)/shard_map/while/body/eval_jaxpr/cond/branch_1_fun/hgqk,khd->hgqd/dot_general | solution.py:38
  397.3 53.2 %conditional.3 = ((f32[4,8,512]{2,1,0:T(8,128)S(1)}, f32[4,8,512]{2,1,0:T(8,128)S(1)}, f32[4,8,512,128]{3,2,1,0:T(8,128)})) conditional(s32[]{:T(128)} %convert_element_type.73, (f32[4,8,512]{2,1,0:T(8,128)S(1)}, f32[4,8,512]{2,1,0:T(8,128)S(1)}, f32[4,8,512,128]{3,2,1,0:T(8,128)}) %tuple.65, (s32[]{:T(128)}, s32[]{:T(128)}, ...), branch_computations={%region_7.7_spmd, %region_8.10_spmd} | conditional | flops 4409319936 | bytes 185665888 | solution.py:62
  430.4 16.9 %multiply_add_fusion = f32[4,8,512,128]{3,2,1,0:T(8,128)S(1)} fusion(f32[4,8,512,128]{3,2,1,0:T(8,128)S(1)} %bitcast.86, f32[4,8,512]{2,1,0:T(8,128)S(1)} %get-tuple-element.367, bf16[512,4,128,1]{0,2,3,1:T(8,128)(2,1)S(1)} %bitcast.88, f32[4,512,512,8]{2,1,3,0:T(8,128)} %get-tuple-element.378, f32[4,8,512]{2,1,0:T(8,128)S(1)} %max.21, ...), kind=kOutput, calls=%fused_computation.11 | convolution fusion | flops 2193620992 | bytes 51249152 | tf_op jit(solution)/shard_map/while/body/eval_jaxpr/cond/branch_1_fun/hgqk,khd->hgqd/dot_general | solution.py:38
  451.1 53.2 %conditional.3 = ((f32[4,8,512]{2,1,0:T(8,128)S(1)}, f32[4,8,512]{2,1,0:T(8,128)S(1)}, f32[4,8,512,128]{3,2,1,0:T(8,128)})) conditional(s32[]{:T(128)} %convert_element_type.73, (f32[4,8,512]{2,1,0:T(8,128)S(1)}, f32[4,8,512]{2,1,0:T(8,128)S(1)}, f32[4,8,512,128]{3,2,1,0:T(8,128)}) %tuple.65, (s32[]{:T(128)}, s32[]{:T(128)}, ...), branch_computations={%region_7.7_spmd, %region_8.10_spmd} | conditional | flops 4409319936 | bytes 185665888 | solution.py:62
  484.2 16.9 %multiply_add_fusion = f32[4,8,512,128]{3,2,1,0:T(8,128)S(1)} fusion(f32[4,8,512,128]{3,2,1,0:T(8,128)S(1)} %bitcast.86, f32[4,8,512]{2,1,0:T(8,128)S(1)} %get-tuple-element.367, bf16[512,4,128,1]{0,2,3,1:T(8,128)(2,1)S(1)} %bitcast.88, f32[4,512,512,8]{2,1,3,0:T(8,128)} %get-tuple-element.378, f32[4,8,512]{2,1,0:T(8,128)S(1)} %max.21, ...), kind=kOutput, calls=%fused_computation.11 | convolution fusion | flops 2193620992 | bytes 51249152 | tf_op jit(solution)/shard_map/while/body/eval_jaxpr/cond/branch_1_fun/hgqk,khd->hgqd/dot_general | solution.py:38
  505.0 53.3 %conditional.3 = ((f32[4,8,512]{2,1,0:T(8,128)S(1)}, f32[4,8,512]{2,1,0:T(8,128)S(1)}, f32[4,8,512,128]{3,2,1,0:T(8,128)})) conditional(s32[]{:T(128)} %convert_element_type.73, (f32[4,8,512]{2,1,0:T(8,128)S(1)}, f32[4,8,512]{2,1,0:T(8,128)S(1)}, f32[4,8,512,128]{3,2,1,0:T(8,128)}) %tuple.65, (s32[]{:T(128)}, s32[]{:T(128)}, ...), branch_computations={%region_7.7_spmd, %region_8.10_spmd} | conditional | flops 4409319936 | bytes 185665888 | solution.py:62
  506.9 16.1 %fusion.2 = (f32[4,8,512]{2,1,0:T(8,128)S(1)}, f32[4,512,512,8]{2,1,3,0:T(8,128)}) fusion(pred[512,512]{0,1:T(8,128)(4,1)S(1)} %fusion.10, bf16[512,4,128,1]{0,2,3,1:T(8,128)(2,1)S(1)} %bitcast.84, bf16[512,4,8,128]{3,0,2,1:T(8,128)(2,1)} %get-tuple-element.265), kind=kOutput, calls=%fused_computation.6 | convolution fusion | flops 2172633088 | bytes 38600704 | tf_op jit(solution)/shard_map/while/body/eval_jaxpr/cond/branch_1_fun/qhgd,khd->hgqk/dot_general | solution.py:21
  538.1 16.9 %multiply_add_fusion = f32[4,8,512,128]{3,2,1,0:T(8,128)S(1)} fusion(f32[4,8,512,128]{3,2,1,0:T(8,128)S(1)} %bitcast.86, f32[4,8,512]{2,1,0:T(8,128)S(1)} %get-tuple-element.367, bf16[512,4,128,1]{0,2,3,1:T(8,128)(2,1)S(1)} %bitcast.88, f32[4,512,512,8]{2,1,3,0:T(8,128)} %get-tuple-element.378, f32[4,8,512]{2,1,0:T(8,128)S(1)} %max.21, ...), kind=kOutput, calls=%fused_computation.11 | convolution fusion | flops 2193620992 | bytes 51249152 | tf_op jit(solution)/shard_map/while/body/eval_jaxpr/cond/branch_1_fun/hgqk,khd->hgqd/dot_general | solution.py:38
  558.9 53.3 %conditional.3 = ((f32[4,8,512]{2,1,0:T(8,128)S(1)}, f32[4,8,512]{2,1,0:T(8,128)S(1)}, f32[4,8,512,128]{3,2,1,0:T(8,128)})) conditional(s32[]{:T(128)} %convert_element_type.73, (f32[4,8,512]{2,1,0:T(8,128)S(1)}, f32[4,8,512]{2,1,0:T(8,128)S(1)}, f32[4,8,512,128]{3,2,1,0:T(8,128)}) %tuple.65, (s32[]{:T(128)}, s32[]{:T(128)}, ...), branch_computations={%region_7.7_spmd, %region_8.10_spmd} | conditional | flops 4409319936 | bytes 185665888 | solution.py:62
  560.8 16.1 %fusion.2 = (f32[4,8,512]{2,1,0:T(8,128)S(1)}, f32[4,512,512,8]{2,1,3,0:T(8,128)}) fusion(pred[512,512]{0,1:T(8,128)(4,1)S(1)} %fusion.10, bf16[512,4,128,1]{0,2,3,1:T(8,128)(2,1)S(1)} %bitcast.84, bf16[512,4,8,128]{3,0,2,1:T(8,128)(2,1)} %get-tuple-element.265), kind=kOutput, calls=%fused_computation.6 | convolution fusion | flops 2172633088 | bytes 38600704 | tf_op jit(solution)/shard_map/while/body/eval_jaxpr/cond/branch_1_fun/qhgd,khd->hgqk/dot_general | solution.py:21
  592.0 16.9 %multiply_add_fusion = f32[4,8,512,128]{3,2,1,0:T(8,128)S(1)} fusion(f32[4,8,512,128]{3,2,1,0:T(8,128)S(1)} %bitcast.86, f32[4,8,512]{2,1,0:T(8,128)S(1)} %get-tuple-element.367, bf16[512,4,128,1]{0,2,3,1:T(8,128)(2,1)S(1)} %bitcast.88, f32[4,512,512,8]{2,1,3,0:T(8,128)} %get-tuple-element.378, f32[4,8,512]{2,1,0:T(8,128)S(1)} %max.21, ...), kind=kOutput, calls=%fused_computation.11 | convolution fusion | flops 2193620992 | bytes 51249152 | tf_op jit(solution)/shard_map/while/body/eval_jaxpr/cond/branch_1_fun/hgqk,khd->hgqd/dot_general | solution.py:38
  612.8 53.2 %conditional.3 = ((f32[4,8,512]{2,1,0:T(8,128)S(1)}, f32[4,8,512]{2,1,0:T(8,128)S(1)}, f32[4,8,512,128]{3,2,1,0:T(8,128)})) conditional(s32[]{:T(128)} %convert_element_type.73, (f32[4,8,512]{2,1,0:T(8,128)S(1)}, f32[4,8,512]{2,1,0:T(8,128)S(1)}, f32[4,8,512,128]{3,2,1,0:T(8,128)}) %tuple.65, (s32[]{:T(128)}, s32[]{:T(128)}, ...), branch_computations={%region_7.7_spmd, %region_8.10_spmd} | conditional | flops 4409319936 | bytes 185665888 | solution.py:62
  645.9 16.9 %multiply_add_fusion = f32[4,8,512,128]{3,2,1,0:T(8,128)S(1)} fusion(f32[4,8,512,128]{3,2,1,0:T(8,128)S(1)} %bitcast.86, f32[4,8,512]{2,1,0:T(8,128)S(1)} %get-tuple-element.367, bf16[512,4,128,1]{0,2,3,1:T(8,128)(2,1)S(1)} %bitcast.88, f32[4,512,512,8]{2,1,3,0:T(8,128)} %get-tuple-element.378, f32[4,8,512]{2,1,0:T(8,128)S(1)} %max.21, ...), kind=kOutput, calls=%fused_computation.11 | convolution fusion | flops 2193620992 | bytes 51249152 | tf_op jit(solution)/shard_map/while/body/eval_jaxpr/cond/branch_1_fun/hgqk,khd->hgqd/dot_general | solution.py:38
  (194 shorter events, 299.0 us)
Async XLA Ops:
  6.5 161.6 %copy-start = (s32[1,128,128]{2,1,0:T(8,128)S(1)}, s32[1,128,128]{2,1,0:T(8,128)}, u32[]{:S(2)}) copy-start(s32[1,128,128]{2,1,0:T(8,128)} %param.17) | copy-start | bytes 196612
  6.5 116.5 %all-gather.3.cloned.1.call-start = ((), (), s32[]{:S(2)}) async-start(), calls=%async_computation.1 | async-start | bytes 17825792 | tf_op jit(solution)/shard_map/all_gather | solution.py:82
  11.7 120.2 %copy-start.3 = (bf16[1,256,1024]{2,1,0:T(8,128)(2,1)S(1)}, bf16[1,256,1024]{2,1,0:T(8,128)(2,1)}, u32[]{:S(2)}) copy-start(bf16[1,256,1024]{2,1,0:T(8,128)(2,1)} %param.14) | copy-start | bytes 1572868
  134.2 30.2 %all-to-all-start = ((bf16[16,64,1024]{2,1,0:T(8,128)(2,1)}), bf16[16,64,1024]{2,1,0:T(8,128)(2,1)S(1)}, u32[]{:S(2)}, u32[]{:S(2)}) async-start(bf16[16,64,1024]{2,1,0:T(8,128)(2,1)} %bitcast_select_fusion.1), calls=%async_computation | async-start | bytes 4194304 | tf_op jit(solution)/shard_map/all_to_all | solution.py:101
  139.4 80.0 %all-gather.5.cloned.1.call-start = ((), (), s32[]{:S(2)}) async-start(), calls=%async_computation.2 | async-start | bytes 9437184 | tf_op jit(solution)/shard_map/all_gather | solution.py:138
  236.1 32.6 %slice-start = ((s8[8388608]{0:T(1024)(128)(4,1)}), s8[4194304]{0:T(1024)(128)(4,1)S(1)}, s32[]{:S(2)}) async-start(s8[8388608]{0:T(1024)(128)(4,1)} %bitcast.85), calls=%async_computation.3 | async-start | bytes 8388608 | tf_op jit(solution)/shard_map/while/body/eval_jaxpr/cond
  237.5 31.2 %slice-start.1 = ((s8[8388608]{0:T(1024)(128)(4,1)}), s8[4194304]{0:T(1024)(128)(4,1)S(1)}, s32[]{:S(2)}) async-start(s8[8388608]{0:T(1024)(128)(4,1)} %bitcast.85), calls=%async_computation.4 | async-start | bytes 8388608 | tf_op jit(solution)/shard_map/while/body/eval_jaxpr/cond
  285.7 3.2 copy-start.2
  290.0 32.6 %slice-start = ((s8[8388608]{0:T(1024)(128)(4,1)}), s8[4194304]{0:T(1024)(128)(4,1)S(1)}, s32[]{:S(2)}) async-start(s8[8388608]{0:T(1024)(128)(4,1)} %bitcast.85), calls=%async_computation.3 | async-start | bytes 8388608 | tf_op jit(solution)/shard_map/while/body/eval_jaxpr/cond
  291.4 31.2 %slice-start.1 = ((s8[8388608]{0:T(1024)(128)(4,1)}), s8[4194304]{0:T(1024)(128)(4,1)S(1)}, s32[]{:S(2)}) async-start(s8[8388608]{0:T(1024)(128)(4,1)} %bitcast.85), calls=%async_computation.4 | async-start | bytes 8388608 | tf_op jit(solution)/shard_map/while/body/eval_jaxpr/cond
  339.6 3.2 copy-start.2
  343.8 32.6 %slice-start = ((s8[8388608]{0:T(1024)(128)(4,1)}), s8[4194304]{0:T(1024)(128)(4,1)S(1)}, s32[]{:S(2)}) async-start(s8[8388608]{0:T(1024)(128)(4,1)} %bitcast.85), calls=%async_computation.3 | async-start | bytes 8388608 | tf_op jit(solution)/shard_map/while/body/eval_jaxpr/cond
  345.3 31.2 %slice-start.1 = ((s8[8388608]{0:T(1024)(128)(4,1)}), s8[4194304]{0:T(1024)(128)(4,1)S(1)}, s32[]{:S(2)}) async-start(s8[8388608]{0:T(1024)(128)(4,1)} %bitcast.85), calls=%async_computation.4 | async-start | bytes 8388608 | tf_op jit(solution)/shard_map/while/body/eval_jaxpr/cond
  397.7 32.6 %slice-start = ((s8[8388608]{0:T(1024)(128)(4,1)}), s8[4194304]{0:T(1024)(128)(4,1)S(1)}, s32[]{:S(2)}) async-start(s8[8388608]{0:T(1024)(128)(4,1)} %bitcast.85), calls=%async_computation.3 | async-start | bytes 8388608 | tf_op jit(solution)/shard_map/while/body/eval_jaxpr/cond
  399.2 31.2 %slice-start.1 = ((s8[8388608]{0:T(1024)(128)(4,1)}), s8[4194304]{0:T(1024)(128)(4,1)S(1)}, s32[]{:S(2)}) async-start(s8[8388608]{0:T(1024)(128)(4,1)} %bitcast.85), calls=%async_computation.4 | async-start | bytes 8388608 | tf_op jit(solution)/shard_map/while/body/eval_jaxpr/cond
  451.6 32.6 %slice-start = ((s8[8388608]{0:T(1024)(128)(4,1)}), s8[4194304]{0:T(1024)(128)(4,1)S(1)}, s32[]{:S(2)}) async-start(s8[8388608]{0:T(1024)(128)(4,1)} %bitcast.85), calls=%async_computation.3 | async-start | bytes 8388608 | tf_op jit(solution)/shard_map/while/body/eval_jaxpr/cond
  453.0 31.2 %slice-start.1 = ((s8[8388608]{0:T(1024)(128)(4,1)}), s8[4194304]{0:T(1024)(128)(4,1)S(1)}, s32[]{:S(2)}) async-start(s8[8388608]{0:T(1024)(128)(4,1)} %bitcast.85), calls=%async_computation.4 | async-start | bytes 8388608 | tf_op jit(solution)/shard_map/while/body/eval_jaxpr/cond
  505.5 32.6 %slice-start = ((s8[8388608]{0:T(1024)(128)(4,1)}), s8[4194304]{0:T(1024)(128)(4,1)S(1)}, s32[]{:S(2)}) async-start(s8[8388608]{0:T(1024)(128)(4,1)} %bitcast.85), calls=%async_computation.3 | async-start | bytes 8388608 | tf_op jit(solution)/shard_map/while/body/eval_jaxpr/cond
  506.9 31.2 %slice-start.1 = ((s8[8388608]{0:T(1024)(128)(4,1)}), s8[4194304]{0:T(1024)(128)(4,1)S(1)}, s32[]{:S(2)}) async-start(s8[8388608]{0:T(1024)(128)(4,1)} %bitcast.85), calls=%async_computation.4 | async-start | bytes 8388608 | tf_op jit(solution)/shard_map/while/body/eval_jaxpr/cond
  559.3 32.6 %slice-start = ((s8[8388608]{0:T(1024)(128)(4,1)}), s8[4194304]{0:T(1024)(128)(4,1)S(1)}, s32[]{:S(2)}) async-start(s8[8388608]{0:T(1024)(128)(4,1)} %bitcast.85), calls=%async_computation.3 | async-start | bytes 8388608 | tf_op jit(solution)/shard_map/while/body/eval_jaxpr/cond
  560.8 31.2 %slice-start.1 = ((s8[8388608]{0:T(1024)(128)(4,1)}), s8[4194304]{0:T(1024)(128)(4,1)S(1)}, s32[]{:S(2)}) async-start(s8[8388608]{0:T(1024)(128)(4,1)} %bitcast.85), calls=%async_computation.4 | async-start | bytes 8388608 | tf_op jit(solution)/shard_map/while/body/eval_jaxpr/cond
  613.2 32.6 %slice-start = ((s8[8388608]{0:T(1024)(128)(4,1)}), s8[4194304]{0:T(1024)(128)(4,1)S(1)}, s32[]{:S(2)}) async-start(s8[8388608]{0:T(1024)(128)(4,1)} %bitcast.85), calls=%async_computation.3 | async-start | bytes 8388608 | tf_op jit(solution)/shard_map/while/body/eval_jaxpr/cond
  614.7 31.2 %slice-start.1 = ((s8[8388608]{0:T(1024)(128)(4,1)}), s8[4194304]{0:T(1024)(128)(4,1)S(1)}, s32[]{:S(2)}) async-start(s8[8388608]{0:T(1024)(128)(4,1)} %bitcast.85), calls=%async_computation.4 | async-start | bytes 8388608 | tf_op jit(solution)/shard_map/while/body/eval_jaxpr/cond
  666.0 17.2 %copy-start.1 = (s32[1,128,128]{2,1,0:T(8,128)S(1)}, s32[1,128,128]{2,1,0:T(8,128)}, u32[]{:S(2)}) copy-start(s32[1,128,128]{2,1,0:T(8,128)} %param.17) | copy-start | bytes 196612
  (6 other events, 19.1 us)
Sparse Core Ops, SparseCore 0:
  9.5 113.5 all-gather.2
  167.6 51.7 all-gather.4
where the time goes:
time: 693 us; the launch traced here: 690 us
  matrix products  273 us (39%)
  waiting for transfers between devices  172 us (25%)
  other arithmetic  139 us (20%)
  local copies, waits for them, and re-layouts  80.6 us (12%)
  between operations  13.6 us (2%)
    dot_general x8, matrix products, head_update(): jnp.einsum('hgqk,khd->hgqd', weights.astype(jnp.bfloat16), value_rows, pr...  135 us
    dot_general x8, matrix products, head_update(): jnp.einsum('qhgd,khd->hgqk', query_rows, key_rows, preferred_element_type...  128 us
    reduce_sum x8, other arithmetic, head_update(): denominator = denominator * factor + jnp.sum(weights, axis=-1)  120 us
    all_gather x1, waiting for transfers between devices, body(): lax.all_gather(w_kv, 'pool', axis=0, tiled=True)  111 us
    all_gather x1, waiting for transfers between devices, body(): key_piece = lax.all_gather(assembled, 'seq', axis=0, tiled=True)  37 us
    cond x56, local copies, waits for them, and re-layouts  25.6 us
    unnamed x10, local copies, waits for them, and re-layouts  24.3 us
    all_to_all x1, waiting for transfers between devices, body(): lax.all_to_all(sending, 'pool', split_axis=0, concat_axis=0, tiled=True)  23.1 us
  transfers between devices with their start and end apart: 3, of which 3 were waited for; matrix products, arithmetic and copies ran while one was open for 3% of the time, Pallas kernels for 0%

commit v1 on v0

v1 whole, which is shorter than its diff:
```python
import functools
import jax
import jax.numpy as jnp
from jax import lax
from jax.experimental import pallas as pl
from jax.experimental.pallas import tpu as pltpu
from jax.sharding import PartitionSpec as P

HEAD_SIZE = 128
BLOCK_ROWS = 32
SOURCE_CAP = 2
CHUNK = 512
KEY_TILE = 1024
SEQ_BLOCKS = 128
NEGATIVE = -1e30
EPS_NORM = 1e-06
LOG2_SCALE = HEAD_SIZE**-0.5 * 1.4426950408889634

bf16 = jnp.bfloat16
f32 = jnp.float32


def matmul(a, b):
    return lax.dot_general(a, b, (((1,), (0,)), ((), ())), preferred_element_type=f32)


def iota(shape, dim):
    return lax.broadcasted_iota(jnp.int32, shape, dim)


def build_keys(k_ref, v_ref, mask_ref, keys, values):
    square = (SEQ_BLOCKS, SEQ_BLOCKS)
    query_block, key_block = iota(square, 0), iota(square, 1)
    allowed = ((mask_ref[...] == 1) & (key_block < query_block)) | (key_block == query_block)
    bias = jnp.where(allowed, 0.0, NEGATIVE).astype(bf16)
    per_chunk = CHUNK // BLOCK_ROWS
    for t in range(k_ref.shape[0] // CHUNK):
        rows = slice(t * CHUNK, (t + 1) * CHUNK)
        spread = iota((SEQ_BLOCKS, CHUNK), 1) // BLOCK_ROWS + t * per_chunk
        spread = (spread == iota((SEQ_BLOCKS, CHUNK), 0)).astype(bf16)
        keys[0:HEAD_SIZE, rows] = k_ref[rows, :].T
        keys[HEAD_SIZE:, rows] = matmul(bias, spread).astype(bf16)
        values[rows, 0:HEAD_SIZE] = v_ref[rows, :]
        values[rows, HEAD_SIZE:] = jnp.ones((CHUNK, HEAD_SIZE), bf16)


def attention_kernel(q_ref, k_ref, v_ref, mask_ref, o_ref, keys, values, rows, maxima, total):
    chunk = pl.program_id(0)
    heads = q_ref.shape[2] // HEAD_SIZE

    @pl.when(chunk == 0)
    def _():
        build_keys(k_ref, v_ref, mask_ref, keys, values)

    square = (CHUNK, SEQ_BLOCKS)
    one_hot = iota(square, 0) // BLOCK_ROWS + chunk * (CHUNK // BLOCK_ROWS)
    one_hot = (one_hot == iota(square, 1)).astype(bf16)
    for h in range(heads):
        rows[h, :, 0:HEAD_SIZE] = q_ref[0, :, h * HEAD_SIZE : (h + 1) * HEAD_SIZE]
        rows[h, :, HEAD_SIZE:] = one_hot
    maxima[...] = jnp.full(maxima.shape, NEGATIVE, f32)
    total[...] = jnp.zeros(total.shape, f32)

    def tile(h, start, width, diagonal):
        scores = matmul(rows[h], keys[:, pl.ds(start, width)])
        if diagonal:
            shape = (CHUNK, width)
            scores = jnp.where(iota(shape, 1) <= iota(shape, 0), scores, NEGATIVE)
        old_max = maxima[h]
        new_max = jnp.maximum(old_max, jnp.max(scores, axis=1, keepdims=True))
        wide_max = jnp.concatenate([new_max] * (width // HEAD_SIZE), axis=1)
        weights = jnp.exp2((scores - wide_max) * LOG2_SCALE)
        factor = jnp.exp2((old_max - new_max) * LOG2_SCALE)
        maxima[h] = new_max
        added = matmul(weights.astype(bf16), values[pl.ds(start, width), :])
        total[h] = total[h] * jnp.concatenate([factor, factor], axis=1) + added

    def step(index, carry):
        for h in range(heads):
            tile(h, pl.multiple_of(index * KEY_TILE, KEY_TILE), KEY_TILE, False)
        return carry

    full = chunk * CHUNK // KEY_TILE
    lax.fori_loop(0, full, step, 0)

    @pl.when(chunk * CHUNK % KEY_TILE != 0)
    def _():
        for h in range(heads):
            tile(h, pl.multiple_of(full * KEY_TILE, CHUNK), CHUNK, False)

    for h in range(heads):
        tile(h, pl.multiple_of(chunk * CHUNK, CHUNK), CHUNK, True)
    for h in range(heads):
        summed = total[h]
        result = summed[:, 0:HEAD_SIZE] / summed[:, HEAD_SIZE:]
        o_ref[0, :, h * HEAD_SIZE : (h + 1) * HEAD_SIZE] = result.astype(bf16)


def attention(q, k, v, mask):
    chunks, _, width = q.shape
    heads = width // HEAD_SIZE
    tokens = k.shape[0]
    chunk_spec = pl.BlockSpec((1, CHUNK, width), lambda i: (i, 0, 0))
    key_spec = pl.BlockSpec((tokens, HEAD_SIZE), lambda i: (0, 0))
    return pl.pallas_call(
        attention_kernel,
        grid=(chunks,),
        in_specs=[
            chunk_spec,
            key_spec,
            key_spec,
            pl.BlockSpec((SEQ_BLOCKS, SEQ_BLOCKS), lambda i: (0, 0)),
        ],
        out_specs=chunk_spec,
        out_shape=jax.ShapeDtypeStruct(q.shape, bf16),
        scratch_shapes=[
            pltpu.VMEM((2 * HEAD_SIZE, tokens), bf16),
            pltpu.VMEM((tokens, 2 * HEAD_SIZE), bf16),
            pltpu.VMEM((heads, CHUNK, 2 * HEAD_SIZE), bf16),
            pltpu.VMEM((heads, CHUNK, HEAD_SIZE), f32),
            pltpu.VMEM((heads, CHUNK, 2 * HEAD_SIZE), f32),
        ],
        compiler_params=pltpu.CompilerParams(vmem_limit_bytes=40 * 2**20),
        cost_estimate=pl.CostEstimate(
            flops=40 * 10**9, bytes_accessed=12 * 2**20, transcendentals=36 * 2**20
        ),
    )(q, k, v, mask)


def swap_cores(x):
    count = lax.axis_size("seq")
    return lax.ppermute(x, "seq", [(i, i ^ 1) for i in range(count)])


def encode(tile_embeds, w_kv, core):
    tiles = tile_embeds.astype(f32)
    mean_square = jnp.mean(tiles * tiles, axis=-1, keepdims=True)
    normed = (tiles * lax.rsqrt(mean_square + EPS_NORM)).astype(bf16)
    half = w_kv.shape[1] // 2
    columns = lax.dynamic_slice_in_dim(w_kv, core * half, half, 1)
    columns = lax.all_gather(columns, "pool", axis=0, tiled=True)
    other = swap_cores(normed)
    mine = jnp.dot(normed, columns, preferred_element_type=f32).astype(bf16)
    theirs = jnp.dot(other, columns, preferred_element_type=f32).astype(bf16)
    arrived = swap_cores(theirs)
    return jnp.where(
        core == 0,
        jnp.concatenate([mine, arrived], axis=1),
        jnp.concatenate([arrived, mine], axis=1),
    )


def body(queries, text_kv, tile_embeds, stored_kv, w_kv, block_source, block_mask):
    pool_count = lax.axis_size("pool")
    seq_count = lax.axis_size("seq")
    my_pool = lax.axis_index("pool")
    my_seq = lax.axis_index("seq")
    core = my_seq % 2
    tokens = queries.shape[1]
    width = text_kv.shape[2]
    shard_blocks = tokens // BLOCK_ROWS
    store_slots = stored_kv.shape[1] // BLOCK_ROWS
    tile_slots = tile_embeds.shape[1] // BLOCK_ROWS
    entries = store_slots + tile_slots

    by_heads = queries[0].reshape(tokens, seq_count, -1).transpose(1, 0, 2)
    by_heads = lax.all_to_all(by_heads, "seq", split_axis=0, concat_axis=0, tiled=True)

    encoded = encode(tile_embeds[0], w_kv, core).reshape(tile_slots, BLOCK_ROWS, width)
    block_table = jnp.concatenate(
        [stored_kv[0].reshape(store_slots, BLOCK_ROWS, width), encoded], axis=0
    )

    is_image = block_source > 0
    source_index = jnp.maximum(block_source - 1, 0)
    source_pool = source_index // entries
    entry_index = source_index % entries
    outgoing = is_image & (source_pool == my_pool)
    order_rank = jnp.cumsum(outgoing.astype(jnp.int32), axis=1) - 1
    slot_ids = lax.iota(jnp.int32, SOURCE_CAP)
    selected = outgoing[:, None, :] & (order_rank[:, None, :] == slot_ids[None, :, None])
    picked_entry = jnp.sum(jnp.where(selected, entry_index[:, None, :], 0), axis=2)
    sending = jnp.take(block_table, picked_entry.reshape(-1), axis=0, mode="clip")
    sending = sending.reshape(-1, width)
    arrived = lax.all_to_all(sending, "pool", split_axis=0, concat_axis=0, tiled=True)
    arrived = arrived.reshape(pool_count * SOURCE_CAP, BLOCK_ROWS, width)

    my_codes = lax.dynamic_index_in_dim(block_source, my_pool, 0, keepdims=False)
    my_image = my_codes > 0
    my_source = jnp.maximum(my_codes - 1, 0) // entries
    block_order = lax.iota(jnp.int32, shard_blocks)
    same_source = (
        my_image[None, :]
        & (my_source[None, :] == my_source[:, None])
        & (block_order[None, :] < block_order[:, None])
    )
    my_rank = jnp.sum(same_source.astype(jnp.int32), axis=1)
    fetched = jnp.take(arrived, my_source * SOURCE_CAP + my_rank, axis=0, mode="clip")
    local_blocks = text_kv[0].reshape(shard_blocks, BLOCK_ROWS, width)
    assembled = jnp.where(my_image[:, None, None], fetched, local_blocks)

    parts = assembled.reshape(tokens, 2, seq_count // 2, HEAD_SIZE).transpose(2, 1, 0, 3)
    parts = parts.reshape(seq_count * tokens, HEAD_SIZE)
    half = lax.all_to_all(parts, "seq", split_axis=0, concat_axis=0, tiled=True)
    other = swap_cores(half)
    keys = jnp.where(core == 0, half, other)
    values = jnp.where(core == 0, other, half)

    attended = attention(by_heads, keys, values, block_mask[0])
    attended = lax.all_to_all(attended, "seq", split_axis=0, concat_axis=0, tiled=True)
    return attended.transpose(1, 0, 2).reshape(1, tokens, -1)


def solution(mesh):
    return jax.shard_map(
        body,
        mesh=mesh,
        in_specs=(
            P("pool", "seq", None),
            P("pool", "seq", None),
            P("seq", "pool", None),
            P("seq", "pool", None),
            P("pool", None),
            P(None, "seq"),
            P("pool", None, None),
        ),
        out_specs=P("pool", "seq", None),
        check_vma=False,
    )
```

time: 693 us -> 347 us (0.50)
  matrix products: 273 us -> 6.8 us
  other arithmetic: 139 us -> 9.37 us
  Pallas kernels: 0 us -> 62 us
  blocking collectives: 0 us -> 53.4 us
  local copies, waits for them, and re-layouts: 80.6 us -> 37.3 us
  waiting for transfers between devices: 172 us -> 136 us
  starting transfers between devices: 5.24 us -> 22.3 us
    dot_general x17 -> x2, matrix products: 273 us -> 6.8 us  [the longest x1 5.42 us: encode(): theirs = jnp.dot(other, columns, preferred_element_type=f32).astype(bf16)]
    reduce_sum x9 -> x1, other arithmetic: 122 us -> 2.08 us  [encode(): mean_square = jnp.mean(tiles * tiles, axis=-1, keepdims=True)]
    all_gather x2 -> x1, waiting for transfers between devices: 148 us -> 65 us  [encode(): columns = lax.all_gather(columns, 'pool', axis=0, tiled=True)]
    pallas_call x0 -> x1, Pallas kernels: none -> 62 us  [attention(): pl.pallas_call(attention_kernel, grid=(chunks,), in_specs=[chunk_spec, ke...]
    all_to_all x0 -> x1, blocking collectives: none -> 53.4 us  [body(): lax.all_to_all(attended, 'seq', split_axis=0, concat_axis=0, tiled=True)]
    all_to_all x0 -> x2, waiting for transfers between devices: none -> 43.1 us  [the longest x1 42.5 us: body(): lax.all_to_all(by_heads, 'seq', split_axis=0, concat_axis=0, tiled=True)]
    cond x56 -> x0, local copies, waits for them, and re-layouts: 25.6 us -> none
    unnamed x10 -> x13, local copies, waits for them, and re-layouts: 24.3 us -> 7.8 us
  transfers between devices with their start and end apart: 3 -> 7, of which waited for: 3 -> 6; matrix products, arithmetic and copies ran while one was open for 3% -> 7% of each run, Pallas kernels for 0% -> 0%
where the time goes in v1:
time: 347 us; the launch traced here: 341 us
  waiting for transfers between devices  136 us (39%)
  Pallas kernels  62 us (18%)
  blocking collectives  53.4 us (15%)
  local copies, waits for them, and re-layouts  37.3 us (11%)
  starting transfers between devices  22.3 us (6%)
  between operations  13.5 us (4%)
  other arithmetic  9.37 us (3%)
  matrix products  6.8 us (2%)
    all_gather x1, waiting for transfers between devices, encode(): columns = lax.all_gather(columns, 'pool', axis=0, tiled=True)  65 us
    pallas_call x1, Pallas kernels, attention(): pl.pallas_call(attention_kernel, grid=(chunks,), in_specs=[chunk_spec, ke...  62 us
    all_to_all x1, blocking collectives, body(): lax.all_to_all(attended, 'seq', split_axis=0, concat_axis=0, tiled=True)  53.4 us
    all_to_all x1, waiting for transfers between devices, body(): lax.all_to_all(by_heads, 'seq', split_axis=0, concat_axis=0, tiled=True)  42.5 us
    all_to_all x1, waiting for transfers between devices, body(): lax.all_to_all(sending, 'pool', split_axis=0, concat_axis=0, tiled=True)  22 us
    all_to_all x1, starting transfers between devices, body(): half = lax.all_to_all(parts, 'seq', split_axis=0, concat_axis=0, tiled=True)  7.83 us
    unnamed x13, local copies, waits for them, and re-layouts  7.8 us
    all_to_all x1, starting transfers between devices, body(): lax.all_to_all(by_heads, 'seq', split_axis=0, concat_axis=0, tiled=True)  7.05 us
  transfers between devices with their start and end apart: 7, of which 6 were waited for; matrix products, arithmetic and copies ran while one was open for 7% of the time, Pallas kernels for 0%

profile of v1, /device:TPU:27, one launch (start us, length us, event | category | flops | bytes accessed | tf_op | source)
XLA Modules:
  0.0 340.8 jit_solution(1371876415022419316)
XLA Ops:
  8.6 2.1 fusion
  10.7 2.0 fusion.1
  14.0 3.4 collective-permute-done
  17.4 65.0 %all-gather.2.cloned.1.call-done = bf16[8192,512]{1,0:T(8,128)(2,1)} async-done(((bf16[512,512]{1,0:T(8,128)(2,1)}), bf16[8192,512]{1,0:T(8,128)(2,1)}) %all-gather.2.cloned.1.call-update) | async-done | bytes 8388624 | tf_op jit(solution)/shard_map/all_gather | solution.py:141
  82.4 5.4 %convolution_convert_fusion = bf16[128,512]{1,0:T(8,128)(2,1)S(1)} fusion(bf16[128,8192]{1,0:T(8,128)(2,1)} %collective-permute-done, bf16[8192,512]{1,0:T(8,128)(2,1)} %all-gather.2.cloned.1.call-done), kind=kOutput, calls=%fused_computation.6 | convolution fusion | flops 1073807360 | bytes 10616832 | tf_op jit(solution)/shard_map/dot_general | solution.py:144
  88.8 1.4 convolution_convert_fusion.1
  90.4 2.0 gather_fusion
  92.4 5.2 %all-to-all-start.1 = ((bf16[16,64,1024]{2,1,0:T(8,128)(2,1)}), bf16[16,64,1024]{2,1,0:T(8,128)(2,1)S(1)}, u32[]{:S(2)}, u32[]{:S(2)}) async-start(bf16[16,64,1024]{2,1,0:T(8,128)(2,1)} %bitcast.55), calls=%async_computation.1 | async-start | bytes 4194304 | tf_op jit(solution)/shard_map/all_to_all | solution.py:185
  97.8 2.6 reshape_squeeze.11
  100.6 22.0 %all-to-all-done.1 = bf16[16,64,1024]{2,1,0:T(8,128)(2,1)S(1)} async-done(((bf16[16,64,1024]{2,1,0:T(8,128)(2,1)}), bf16[16,64,1024]{2,1,0:T(8,128)(2,1)S(1)}, u32[]{:S(2)}, u32[]{:S(2)}) %all-to-all-start.1) | async-done | bytes 2097184 | tf_op jit(solution)/shard_map/all_to_all | solution.py:185
  122.6 1.6 gather_fusion.1
  124.2 1.8 gather.12
  126.0 3.2 select_bitcast_fusion
  130.3 7.8 %all-to-all-start.2 = ((bf16[8,512,128]{2,1,0:T(8,128)(2,1)}), bf16[8,512,128]{2,1,0:T(8,128)(2,1)S(1)}, u32[]{:S(2)}, u32[]{:S(2)}) async-start(bf16[8,512,128]{2,1,0:T(8,128)(2,1)} %bitcast.18), calls=%async_computation.2 | async-start | bytes 2097152 | tf_op jit(solution)/shard_map/all_to_all | solution.py:204
  138.1 6.4 %copy.14 = bf16[1,512,4096]{1,2,0:T(8,128)(2,1)} copy(bf16[1,512,4096]{2,1,0:T(8,128)(2,1)} %param.7) | data formatting | bytes 8388608 | tf_op args[0]
  144.5 6.5 %copy.15 = bf16[512,8,512]{2,0,1:T(8,128)(2,1)} copy(bf16[512,8,512]{0,2,1:T(8,128)(2,1)} %bitcast.54) | data formatting | bytes 8388608 | tf_op jit(solution)/shard_map/reshape;squeeze | solution.py:166
  151.5 7.1 %all-to-all-start = ((bf16[8,512,512]{2,1,0:T(8,128)(2,1)}), bf16[8,512,512]{2,1,0:T(8,128)(2,1)}, u32[]{:S(2)}, u32[]{:S(2)}) async-start(bf16[8,512,512]{2,1,0:T(8,128)(2,1)} %bitcast.51), calls=%async_computation | async-start | bytes 8388608 | tf_op jit(solution)/shard_map/all_to_all | solution.py:167
  159.2 2.6 collective-permute-done.2
  161.8 1.4 broadcast_select_fusion
  163.2 42.5 %all-to-all-done.q_ref = bf16[8,512,512]{2,1,0:T(8,128)(2,1)} async-done(((bf16[8,512,512]{2,1,0:T(8,128)(2,1)}), bf16[8,512,512]{2,1,0:T(8,128)(2,1)}, u32[]{:S(2)}, u32[]{:S(2)}) %all-to-all-start) | async-done | bytes 4194336 | tf_op jit(solution)/shard_map/all_to_all | solution.py:167
  205.7 62.0 %shard_map.73 = bf16[8,512,512]{2,1,0:T(8,128)(2,1)S(1)} custom-call(bf16[8,512,512]{2,1,0:T(8,128)(2,1)} %all-to-all-done.q_ref, bf16[4096,128]{1,0:T(8,128)(2,1)S(1)} %get-tuple-element.11.k_ref, bf16[4096,128]{1,0:T(8,128)(2,1)S(1)} %get-tuple-element.10.v_ref, s32[128,128]{1,0:T(8,128)S(1)} %bitcast.50), custom_call_target="tpu_custom_call" | custom-call | flops 40000000000 | bytes 12582912 | tf_op jit(solution)/shard_map/pallas_call | solution.py:105
  267.7 53.4 %all_to_all.31 = bf16[8,512,512]{2,1,0:T(8,128)(2,1)} all-to-all(bf16[8,512,512]{2,1,0:T(8,128)(2,1)S(1)} %shard_map.73), channel_id=1, replica_groups=mesh['seq'=8,'pool'=16] {'seq'}, dimensions={0} | all-to-all | bytes 8388608 | tf_op jit(solution)/shard_map/all_to_all | solution.py:210
  321.1 6.5 %copy.18 = bf16[512,8,512]{0,2,1:T(8,128)(2,1)} copy(bf16[512,8,512]{2,0,1:T(8,128)(2,1)} %bitcast.52) | data formatting | bytes 8388608 | tf_op jit(solution)/shard_map/transpose | solution.py:211
  327.6 6.3 %copy.19 = bf16[1,512,4096]{2,1,0:T(8,128)(2,1)} copy(bf16[1,512,4096]{1,2,0:T(8,128)(2,1)} %bitcast.53) | data formatting | bytes 8388608 | tf_op jit(solution)/shard_map/reshape | solution.py:211
  (40 shorter events, 7.1 us)
Async XLA Ops:
  6.5 1.2 copy-start
  6.5 7.0 %copy-start.5 = (s32[16,16]{1,0:T(8,128)S(1)}, s32[16,16]{1,0:T(8,128)}, u32[]{:S(2)}) copy-start(s32[16,16]{1,0:T(8,128)} %param.12) | copy-start | bytes 3076
  6.5 75.9 %all-gather.2.cloned.1.call-start = ((), (), s32[]{:S(2)}) async-start(), calls=%async_computation.4 | async-start | bytes 8912896 | tf_op jit(solution)/shard_map/all_gather | solution.py:141
  12.7 4.7 %collective-permute-start = (bf16[128,8192]{1,0:T(8,128)(2,1)S(1)}, bf16[128,8192]{1,0:T(8,128)(2,1)}, u32[]{:S(2)}, u32[]{:S(2)}) collective-permute-start(bf16[128,8192]{1,0:T(8,128)(2,1)S(1)} %fusion.1), channel_id=1, source_target_pairs={{0,16},{16,0},{32,48},{48,32},{64,80},{80,64},{96,112},{112,96},{1... | collective-permute-start | bytes 6291464 | tf_op jit(solution)/shard_map/ppermute | solution.py:132
  82.4 6.4 %copy-start.2 = (bf16[8192,512]{1,0:T(8,128)(2,1)S(1)}, bf16[8192,512]{1,0:T(8,128)(2,1)}, u32[]{:S(2)}) copy-start(bf16[8192,512]{1,0:T(8,128)(2,1)} %all-gather.2.cloned.1.call-done) | copy-start | bytes 25165828
  87.9 2.5 copy-start.4
  87.9 2.4 collective-permute-start.1
  92.4 30.2 %all-to-all-start.1 = ((bf16[16,64,1024]{2,1,0:T(8,128)(2,1)}), bf16[16,64,1024]{2,1,0:T(8,128)(2,1)S(1)}, u32[]{:S(2)}, u32[]{:S(2)}) async-start(bf16[16,64,1024]{2,1,0:T(8,128)(2,1)} %bitcast.55), calls=%async_computation.1 | async-start | bytes 4194304 | tf_op jit(solution)/shard_map/all_to_all | solution.py:185
  130.3 21.2 %all-to-all-start.2 = ((bf16[8,512,128]{2,1,0:T(8,128)(2,1)}), bf16[8,512,128]{2,1,0:T(8,128)(2,1)S(1)}, u32[]{:S(2)}, u32[]{:S(2)}) async-start(bf16[8,512,128]{2,1,0:T(8,128)(2,1)} %bitcast.18), calls=%async_computation.2 | async-start | bytes 2097152 | tf_op jit(solution)/shard_map/all_to_all | solution.py:204
  151.5 7.1 %copy-start.3 = (bf16[8,512,128]{2,1,0:T(8,128)(2,1)}, bf16[8,512,128]{2,1,0:T(8,128)(2,1)S(1)}, u32[]{:S(2)}) copy-start(bf16[8,512,128]{2,1,0:T(8,128)(2,1)S(1)} %all-to-all-done.2) | copy-start | bytes 3145732
  151.5 54.2 %all-to-all-start = ((bf16[8,512,512]{2,1,0:T(8,128)(2,1)}), bf16[8,512,512]{2,1,0:T(8,128)(2,1)}, u32[]{:S(2)}, u32[]{:S(2)}) async-start(bf16[8,512,512]{2,1,0:T(8,128)(2,1)} %bitcast.51), calls=%async_computation | async-start | bytes 8388608 | tf_op jit(solution)/shard_map/all_to_all | solution.py:167
  158.6 47.2 %copy-start.1 = (s32[1,128,128]{2,1,0:T(8,128)S(1)}, s32[1,128,128]{2,1,0:T(8,128)}, u32[]{:S(2)}) copy-start(s32[1,128,128]{2,1,0:T(8,128)} %param.13) | copy-start | bytes 196612
  158.6 3.3 collective-permute-start.2
Sparse Core Ops, SparseCore 0:
  9.5 72.8 all-gather.1
